TPU v7x, 128 devices: a whole 4x4x4 slice. The times are simulated.
128 devices in a mesh: frame: 16 (over y, x_hi, core), patch: 8 (over z, x_lo).
Axes of the slice: x: 4 (x_hi: 2, x_lo: 2; x = x_hi * 2 + x_lo), y: 4, z: 4, core: 2. Of those that a mesh axis runs over, the one named last changes fastest.
Arguments:
- queries: bfloat16 [32, 2048, 5120], P('frame', 'patch'), may hold values from -6 to 6
- keys: bfloat16 [32, 2048, 5120], P('frame', 'patch'), may hold values from -6 to 6
- values: bfloat16 [32, 2048, 5120], P('frame', 'patch'), may hold values from -6 to 6
- spatial_mask: int32 [32, 28, 16, 16], replicated, may hold values from 0 to 1, as said below
- temporal_mask: int32 [64, 12, 8, 8], replicated, may hold values from 0 to 1, as said below
Outputs:
- attended: bfloat16 [32, 2048, 5120], P('frame', 'patch')
Inputs may be any that keep to these rules, and one draw needn't show every extreme that they name: `spatial_mask`: entries are 0 or 1; every diagonal block is 1. `temporal_mask`: entries are 0 or 1; every diagonal block is 1.
All inputs are finite; a program needn't handle non-finite values.
Results may differ from a plain program's by a relative error of at most 0.0046.
Values may be sent and summed in bfloat16 or wider, within the bound.
A program may use at most 320 MiB of HBM per device.

v0:
```python
import jax
import jax.numpy as jnp
from jax import lax
from jax.sharding import PartitionSpec as P

HD = 128
SH = 28
TH = 12
GP = 32
BLOCK = 128


def attend_item(query, key_rows, value_rows, blocks):
    allowed = jnp.repeat(jnp.repeat(blocks > 0, BLOCK, axis=0), BLOCK, axis=1)
    scores = jnp.einsum("qe,ke->qk", query, key_rows, preferred_element_type=jnp.float32) * HD ** (
        -0.5
    )
    scores = jnp.where(allowed, scores, -jnp.inf)
    top = jnp.max(scores, axis=1, keepdims=True)
    probs = jnp.exp(scores - top)
    total = jnp.sum(probs, axis=1, keepdims=True)
    mixed = jnp.dot(probs.astype(jnp.bfloat16), value_rows, preferred_element_type=jnp.float32)
    return (mixed / total).astype(jnp.bfloat16)


def attend_items(stacked, blocks):

    def single(operands):
        return attend_item(operands[0], operands[1], operands[2], operands[3])

    return lax.map(single, (stacked[0], stacked[1], stacked[2], blocks))


def to_sequence(rows, group_count):
    frames_here = rows.shape[0]
    shaped = rows.reshape(frames_here, group_count, GP, TH, HD).transpose(1, 3, 0, 2, 4)
    return shaped.reshape(group_count, TH, frames_here * GP, HD)


def from_sequence(sequence, frames_here):
    group_count = sequence.shape[0]
    shaped = sequence.reshape(group_count, TH, frames_here, GP, HD).transpose(2, 0, 3, 1, 4)
    return shaped.reshape(frames_here, group_count * GP, TH * HD)


def shards(queries, keys, values, spatial_mask, temporal_mask):
    frames_dev, cells_dev, width = queries.shape
    frame_rank = lax.axis_index("frame")
    patch_rank = lax.axis_index("patch")
    split = SH * HD
    stacked = jnp.stack([queries[:, :, :split], keys[:, :, :split], values[:, :, :split]])
    stacked = stacked.reshape(3, frames_dev, cells_dev, SH, HD).transpose(0, 1, 3, 2, 4)
    stacked = stacked.reshape(3, frames_dev * SH, cells_dev, HD)
    spread = lax.all_to_all(stacked, "patch", split_axis=1, concat_axis=2, tiled=True)
    item_count = spread.shape[1]
    frame_masks = lax.dynamic_slice_in_dim(spatial_mask, frame_rank * frames_dev, frames_dev, 0)
    frame_masks = frame_masks.reshape(frames_dev * SH, frame_masks.shape[2], frame_masks.shape[3])
    item_masks = lax.dynamic_slice_in_dim(frame_masks, patch_rank * item_count, item_count, 0)
    spatial_heads = attend_items(spread, item_masks)
    returned = lax.all_to_all(spatial_heads, "patch", split_axis=1, concat_axis=0, tiled=True)
    spatial_out = (
        returned.reshape(frames_dev, SH, cells_dev, HD)
        .transpose(0, 2, 1, 3)
        .reshape(frames_dev, cells_dev, split)
    )
    group_count = cells_dev // GP
    query_part = queries[:, :, split:]
    key_part = keys[:, :, split:]
    value_part = values[:, :, split:]
    group_masks = lax.dynamic_slice_in_dim(temporal_mask, patch_rank * group_count, group_count, 0)
    block_count = group_masks.shape[2]

    def flatten(rows):
        return to_sequence(rows, group_count).reshape(group_count * TH, frames_dev * GP, HD)

    packed = jnp.stack([flatten(query_part), flatten(key_part), flatten(value_part)])
    regrouped = lax.all_to_all(packed, "frame", split_axis=1, concat_axis=2, tiled=True)
    temporal_count = regrouped.shape[1]
    flat_masks = group_masks.reshape(group_count * TH, block_count, block_count)
    temporal_masks = lax.dynamic_slice_in_dim(
        flat_masks, frame_rank * temporal_count, temporal_count, 0
    )
    temporal_heads = attend_items(regrouped, temporal_masks)
    sent_back = lax.all_to_all(temporal_heads, "frame", split_axis=1, concat_axis=0, tiled=True)
    temporal_out = from_sequence(
        sent_back.reshape(group_count, TH, frames_dev * GP, HD), frames_dev
    )
    return jnp.concatenate([spatial_out, temporal_out], axis=2)


def solution(mesh):
    in_specs = (
        P("frame", "patch", None),
        P("frame", "patch", None),
        P("frame", "patch", None),
        P(),
        P(),
    )
    out_specs = P("frame", "patch", None)
    return jax.shard_map(shards, mesh=mesh, in_specs=in_specs, out_specs=out_specs, check_vma=False)
```

profile of v0, /device:TPU:1, one launch (start us, length us, event | category | flops | bytes accessed | tf_op | source)
XLA Modules:
  0.0 406.1 jit_solution(4527372927960864212)
XLA Ops:
  25.5 8.6 %all-to-all-start.2 = ((bf16[3,96,64,128]{3,2,0,1:T(8,128)(2,1)}), bf16[3,96,64,128]{3,2,0,1:T(8,128)(2,1)}, u32[]{:S(2)}, u32[]{:S(2)}) async-start(bf16[3,96,64,128]{3,2,0,1:T(8,128)(2,1)} %copy.60), calls=%async_computation.2 | async-start | bytes 9437184 | tf_op jit(solution)/shard_map/all_to_all | solution.py:77
  34.1 4.3 %slice.42 = bf16[2,256,3584]{2,1,0:T(8,128)(2,1)} slice(bf16[2,256,5120]{2,1,0:T(8,128)(2,1)} %param.9), slice={[0:2], [0:256], [0:3584]} | slice | bytes 7340032 | tf_op jit(solution)/shard_map/slice | solution.py:51
  38.5 4.2 %slice.43 = bf16[2,256,3584]{2,1,0:T(8,128)(2,1)} slice(bf16[2,256,5120]{2,1,0:T(8,128)(2,1)} %param.10), slice={[0:2], [0:256], [0:3584]} | slice | bytes 7340032 | tf_op jit(solution)/shard_map/slice | solution.py:51
  44.7 5.9 %copy.75 = bf16[2,256,3584]{1,2,0:T(8,128)(2,1)} copy(bf16[2,256,3584]{2,1,0:T(8,128)(2,1)} %slice.42) | data formatting | bytes 7340032
  50.6 6.0 %copy.76 = bf16[2,256,3584]{1,2,0:T(8,128)(2,1)} copy(bf16[2,256,3584]{2,1,0:T(8,128)(2,1)} %slice.43) | data formatting | bytes 7340032
  56.6 5.9 %copy.77 = bf16[2,256,3584]{1,2,0:T(8,128)(2,1)} copy(bf16[2,256,3584]{2,1,0:T(8,128)(2,1)} %slice.44) | data formatting | bytes 7340032
  62.5 9.6 %pad_maximum_fusion = bf16[3,2,256,28,128]{2,4,3,1,0:T(8,128)(2,1)} fusion(bf16[1,2,256,28,128]{2,4,3,1,0:T(8,128)(2,1)} %bitcast.152, bf16[1,2,256,28,128]{2,4,3,1,0:T(8,128)(2,1)} %bitcast.151, bf16[1,2,256,28,128]{2,4,3,1,0:T(8,128)(2,1)} %bitcast.150), kind=kLoop, calls=%fused_computation.42 | loop fusion | flops 11010048 | bytes 22020096 | tf_op jit(solution)/shard_map/stack | solution.py:51
  72.2 14.7 %copy.47 = bf16[3,56,256,128]{3,2,0,1:T(8,128)(2,1)} copy(bf16[3,56,256,128]{2,3,1,0:T(8,128)(2,1)} %bitcast.146) | data formatting | bytes 22020096 | tf_op jit(solution)/shard_map/reshape | solution.py:53
  86.9 3.9 all-to-all-done.2
  90.8 5.4 %all-to-all-start = ((bf16[3,56,256,128]{3,2,0,1:T(8,128)(2,1)}), bf16[3,56,256,128]{3,2,0,1:T(8,128)(2,1)}, u32[]{:S(2)}, u32[]{:S(2)}) async-start(bf16[3,56,256,128]{3,2,0,1:T(8,128)(2,1)} %copy.47), calls=%async_computation | async-start | bytes 22020096 | tf_op jit(solution)/shard_map/all_to_all | solution.py:54
  96.3 4.9 %constant_dynamic-slice_fusion.3 = s32[2,28,16,16]{0,3,2,1:T(8,128)} fusion(s32[32,28,16,16]{0,3,2,1:T(8,128)} %param.12, s32[]{:T(128)S(6)} %select_n.20), kind=kLoop, calls=%fused_computation.48 | loop fusion | bytes 114692 | tf_op jit(solution)/shard_map/dynamic_slice | solution.py:56
  101.1 4.5 %copy.42 = s32[2,28,16,16]{2,3,1,0:T(8,128)S(1)} copy(s32[2,28,16,16]{0,3,2,1:T(8,128)} %constant_dynamic-slice_fusion.3) | data formatting | bytes 114688 | tf_op jit(solution)/shard_map/dynamic_slice | solution.py:56
  112.9 29.1 %while.21 = (s32[]{:T(128)}, bf16[6,1024,128]{2,1,0:T(8,128)(2,1)}, s32[6,8,8]{2,1,0:T(8,128)}, bf16[6,1024,128]{2,1,0:T(8,128)(2,1)S(1)}, bf16[6,1024,128]{2,1,...) while((s32[]{:T(128)}, bf16[6,1024,128]{2,1,0:T(8,128)(2,1)}, s32[6,8,8]{2,1,0:T(8,128)}, ...), condition=%wide.region_7.8_spmd, body=%wide.region_4.7_spmd.sunk | while | flops 545519680 | bytes 13674961 | solution.py:31
  145.9 72.5 %all-to-all-done = bf16[3,56,256,128]{3,2,0,1:T(8,128)(2,1)} async-done(((bf16[3,56,256,128]{3,2,0,1:T(8,128)(2,1)}), bf16[3,56,256,128]{3,2,0,1:T(8,128)(2,1)}, u32[]{:S(2)}, u32[]{:S(2)}) %all-to-all-start) | async-done | bytes 11010080 | tf_op jit(solution)/shard_map/all_to_all | solution.py:54
  218.3 5.6 %all-to-all-start.3 = ((bf16[6,1024,128]{2,0,1:T(8,128)(2,1)}), bf16[6,1024,128]{2,0,1:T(8,128)(2,1)S(1)}, u32[]{:S(2)}, u32[]{:S(2)}) async-start(bf16[6,1024,128]{2,0,1:T(8,128)(2,1)} %copy.65), calls=%async_computation.3 | async-start | bytes 4194304 | tf_op jit(solution)/shard_map/all_to_all | solution.py:84
  223.9 6.2 %copy.48 = bf16[3,56,256,128]{3,2,1,0:T(8,128)(2,1)S(1)} copy(bf16[3,56,256,128]{3,2,0,1:T(8,128)(2,1)} %all-to-all-done) | data formatting | bytes 22020096 | tf_op jit(solution)/shard_map/all_to_all | solution.py:54
  238.3 84.2 %while.20 = (s32[]{:T(128)}, bf16[7,2048,128]{2,1,0:T(8,128)(2,1)}, s32[7,16,16]{1,2,0:T(8,128)S(1)}, bf16[7,2048,128]{2,1,0:T(8,128)(2,1)}, bf16[7,2048,128]{2,...) while((s32[]{:T(128)}, bf16[7,2048,128]{2,1,0:T(8,128)(2,1)}, s32[7,16,16]{1,2,0:T(8,128)S(1)}, ...), condition=%wide.region_3.4_spmd, body=%wide.region_0.3_spmd.sunk | while | flops 2181558528 | bytes 52629072 | solution.py:31
  245.9 4.4 %fusion.53 = bf16[7,2048,128]{2,1,0:T(8,128)(2,1)} fusion(bf16[7,2048,128]{2,1,0:T(8,128)(2,1)} %get-tuple-element.228, s32[]{:T(128)} %get-tuple-element.227, bf16[2048,2048]{0,1:T(8,128)(2,1)S(1)} %get-tuple-element.187, f32[2048]{0:T(1024)S(1)} %get-tuple-element.188, bf16[7,2048,128]{2,1,0:T(8,128)(2,1)} %get-tuple-element.239), kind=kOutput, calls=%fused_computation.8.clone.1 | convolution fusion | flops 1074266112 | bytes 9446400 | tf_op jit(solution)/shard_map/while/body/eval_jaxpr/dot_general | solution.py:22
  257.9 4.4 %fusion.53 = bf16[7,2048,128]{2,1,0:T(8,128)(2,1)} fusion(bf16[7,2048,128]{2,1,0:T(8,128)(2,1)} %get-tuple-element.228, s32[]{:T(128)} %get-tuple-element.227, bf16[2048,2048]{0,1:T(8,128)(2,1)S(1)} %get-tuple-element.187, f32[2048]{0:T(1024)S(1)} %get-tuple-element.188, bf16[7,2048,128]{2,1,0:T(8,128)(2,1)} %get-tuple-element.239), kind=kOutput, calls=%fused_computation.8.clone.1 | convolution fusion | flops 1074266112 | bytes 9446400 | tf_op jit(solution)/shard_map/while/body/eval_jaxpr/dot_general | solution.py:22
  266.0 3.9 fusion.52
  270.0 4.4 %fusion.53 = bf16[7,2048,128]{2,1,0:T(8,128)(2,1)} fusion(bf16[7,2048,128]{2,1,0:T(8,128)(2,1)} %get-tuple-element.228, s32[]{:T(128)} %get-tuple-element.227, bf16[2048,2048]{0,1:T(8,128)(2,1)S(1)} %get-tuple-element.187, f32[2048]{0:T(1024)S(1)} %get-tuple-element.188, bf16[7,2048,128]{2,1,0:T(8,128)(2,1)} %get-tuple-element.239), kind=kOutput, calls=%fused_computation.8.clone.1 | convolution fusion | flops 1074266112 | bytes 9446400 | tf_op jit(solution)/shard_map/while/body/eval_jaxpr/dot_general | solution.py:22
  282.0 4.4 %fusion.53 = bf16[7,2048,128]{2,1,0:T(8,128)(2,1)} fusion(bf16[7,2048,128]{2,1,0:T(8,128)(2,1)} %get-tuple-element.228, s32[]{:T(128)} %get-tuple-element.227, bf16[2048,2048]{0,1:T(8,128)(2,1)S(1)} %get-tuple-element.187, f32[2048]{0:T(1024)S(1)} %get-tuple-element.188, bf16[7,2048,128]{2,1,0:T(8,128)(2,1)} %get-tuple-element.239), kind=kOutput, calls=%fused_computation.8.clone.1 | convolution fusion | flops 1074266112 | bytes 9446400 | tf_op jit(solution)/shard_map/while/body/eval_jaxpr/dot_general | solution.py:22
  294.0 4.4 %fusion.53 = bf16[7,2048,128]{2,1,0:T(8,128)(2,1)} fusion(bf16[7,2048,128]{2,1,0:T(8,128)(2,1)} %get-tuple-element.228, s32[]{:T(128)} %get-tuple-element.227, bf16[2048,2048]{0,1:T(8,128)(2,1)S(1)} %get-tuple-element.187, f32[2048]{0:T(1024)S(1)} %get-tuple-element.188, bf16[7,2048,128]{2,1,0:T(8,128)(2,1)} %get-tuple-element.239), kind=kOutput, calls=%fused_computation.8.clone.1 | convolution fusion | flops 1074266112 | bytes 9446400 | tf_op jit(solution)/shard_map/while/body/eval_jaxpr/dot_general | solution.py:22
  306.0 4.4 %fusion.53 = bf16[7,2048,128]{2,1,0:T(8,128)(2,1)} fusion(bf16[7,2048,128]{2,1,0:T(8,128)(2,1)} %get-tuple-element.228, s32[]{:T(128)} %get-tuple-element.227, bf16[2048,2048]{0,1:T(8,128)(2,1)S(1)} %get-tuple-element.187, f32[2048]{0:T(1024)S(1)} %get-tuple-element.188, bf16[7,2048,128]{2,1,0:T(8,128)(2,1)} %get-tuple-element.239), kind=kOutput, calls=%fused_computation.8.clone.1 | convolution fusion | flops 1074266112 | bytes 9446400 | tf_op jit(solution)/shard_map/while/body/eval_jaxpr/dot_general | solution.py:22
  318.1 4.4 %fusion.53 = bf16[7,2048,128]{2,1,0:T(8,128)(2,1)} fusion(bf16[7,2048,128]{2,1,0:T(8,128)(2,1)} %get-tuple-element.228, s32[]{:T(128)} %get-tuple-element.227, bf16[2048,2048]{0,1:T(8,128)(2,1)S(1)} %get-tuple-element.187, f32[2048]{0:T(1024)S(1)} %get-tuple-element.188, bf16[7,2048,128]{2,1,0:T(8,128)(2,1)} %get-tuple-element.239), kind=kOutput, calls=%fused_computation.8.clone.1 | convolution fusion | flops 1074266112 | bytes 9446400 | tf_op jit(solution)/shard_map/while/body/eval_jaxpr/dot_general | solution.py:22
  322.5 5.8 %copy.52 = bf16[7,2048,128]{2,0,1:T(8,128)(2,1)} copy(bf16[7,2048,128]{2,1,0:T(8,128)(2,1)} %get-tuple-element.69) | data formatting | bytes 7340032 | tf_op jit(solution)/shard_map/while | solution.py:31
  328.3 4.8 %all-to-all-start.1 = ((bf16[7,2048,128]{2,0,1:T(8,128)(2,1)}), bf16[7,2048,128]{2,0,1:T(8,128)(2,1)}, u32[]{:S(2)}, u32[]{:S(2)}) async-start(bf16[7,2048,128]{2,0,1:T(8,128)(2,1)} %copy.52), calls=%async_computation.1 | async-start | bytes 8388608 | tf_op jit(solution)/shard_map/all_to_all | solution.py:60
  338.4 44.0 %all-to-all-done.1 = bf16[7,2048,128]{2,0,1:T(8,128)(2,1)} async-done(((bf16[7,2048,128]{2,0,1:T(8,128)(2,1)}), bf16[7,2048,128]{2,0,1:T(8,128)(2,1)}, u32[]{:S(2)}, u32[]{:S(2)}) %all-to-all-start.1) | async-done | bytes 3670048 | tf_op jit(solution)/shard_map/all_to_all | solution.py:60
  382.4 5.0 %copy.54 = bf16[8,7,256,128]{3,2,1,0:T(8,128)(2,1)} copy(bf16[8,7,256,128]{3,1,2,0:T(8,128)(2,1)} %bitcast.27) | data formatting | bytes 7340032 | tf_op jit(solution)/shard_map/all_to_all | solution.py:60
  387.4 6.0 %copy.55 = bf16[2,256,28,128]{1,3,2,0:T(8,128)(2,1)} copy(bf16[2,256,28,128]{3,1,2,0:T(8,128)(2,1)} %bitcast.149) | data formatting | bytes 7340032 | tf_op jit(solution)/shard_map/transpose | solution.py:63
  393.4 4.7 %pad_maximum_fusion.1 = bf16[2,256,5120]{1,2,0:T(8,128)(2,1)} fusion(bf16[2,256,1536]{1,2,0:T(8,128)(2,1)S(1)} %copy.69, bf16[2,256,3584]{1,2,0:T(8,128)(2,1)} %bitcast.148), kind=kLoop, calls=%fused_computation.43 | loop fusion | flops 10485760 | bytes 10485760 | tf_op jit(solution)/shard_map/concatenate | solution.py:88
  398.1 7.9 %copy.70 = bf16[2,256,5120]{2,1,0:T(8,128)(2,1)} copy(bf16[2,256,5120]{1,2,0:T(8,128)(2,1)} %pad_maximum_fusion.1) | data formatting | bytes 10485760 | tf_op jit(solution)/shard_map/concatenate | solution.py:88
  (110 shorter events, 130.2 us)
Async XLA Ops:
  0.0 105.6 %copy-start = (s32[64,12,8,8]{0,3,2,1:T(8,128)S(1)}, s32[64,12,8,8]{0,3,2,1:T(8,128)}, u32[]{:S(2)}) copy-start(s32[64,12,8,8]{0,3,2,1:T(8,128)} %param.13) | copy-start | bytes 589828
  19.8 1.4 copy-start.2
  19.8 1.9 copy-start.3
  25.5 17.1 %slice-start = ((s8[5242880]{0:T(1024)(128)(4,1)}), s8[1048576]{0:T(1024)(128)(4,1)S(1)}, s32[]{:S(2)}) async-start(s8[5242880]{0:T(1024)(128)(4,1)} %bitcast.167), calls=%async_computation.4 | async-start | bytes 2097152
  25.5 65.3 %all-to-all-start.2 = ((bf16[3,96,64,128]{3,2,0,1:T(8,128)(2,1)}), bf16[3,96,64,128]{3,2,0,1:T(8,128)(2,1)}, u32[]{:S(2)}, u32[]{:S(2)}) async-start(bf16[3,96,64,128]{3,2,0,1:T(8,128)(2,1)} %copy.60), calls=%async_computation.2 | async-start | bytes 9437184 | tf_op jit(solution)/shard_map/all_to_all | solution.py:77
  34.1 8.5 %slice-start.1 = ((s8[5242880]{0:T(1024)(128)(4,1)}), s8[4194304]{0:T(1024)(128)(4,1)S(1)}, s32[]{:S(2)}) async-start(s8[5242880]{0:T(1024)(128)(4,1)} %bitcast.167), calls=%async_computation.5 | async-start | bytes 8388608
  90.8 127.5 %all-to-all-start = ((bf16[3,56,256,128]{3,2,0,1:T(8,128)(2,1)}), bf16[3,56,256,128]{3,2,0,1:T(8,128)(2,1)}, u32[]{:S(2)}, u32[]{:S(2)}) async-start(bf16[3,56,256,128]{3,2,0,1:T(8,128)(2,1)} %copy.47), calls=%async_computation | async-start | bytes 22020096 | tf_op jit(solution)/shard_map/all_to_all | solution.py:54
  218.3 110.0 %all-to-all-start.3 = ((bf16[6,1024,128]{2,0,1:T(8,128)(2,1)}), bf16[6,1024,128]{2,0,1:T(8,128)(2,1)S(1)}, u32[]{:S(2)}, u32[]{:S(2)}) async-start(bf16[6,1024,128]{2,0,1:T(8,128)(2,1)} %copy.65), calls=%async_computation.3 | async-start | bytes 4194304 | tf_op jit(solution)/shard_map/all_to_all | solution.py:84
  328.3 54.0 %all-to-all-start.1 = ((bf16[7,2048,128]{2,0,1:T(8,128)(2,1)}), bf16[7,2048,128]{2,0,1:T(8,128)(2,1)}, u32[]{:S(2)}, u32[]{:S(2)}) async-start(bf16[7,2048,128]{2,0,1:T(8,128)(2,1)} %copy.52), calls=%async_computation.1 | async-start | bytes 8388608 | tf_op jit(solution)/shard_map/all_to_all | solution.py:60
  393.4 12.7 %copy-start.1 = (s32[64,12,8,8]{0,3,2,1:T(8,128)S(1)}, s32[64,12,8,8]{0,3,2,1:T(8,128)}, u32[]{:S(2)}) copy-start(s32[64,12,8,8]{0,3,2,1:T(8,128)} %param.13) | copy-start | bytes 589828
where the time goes:
time: 409 us; the launch traced here: 406 us
  local copies, waits for them, and re-layouts  134 us (33%)
  waiting for transfers between devices  120 us (29%)
  matrix products  74.5 us (18%)
  other arithmetic  52.1 us (13%)
  starting transfers between devices  24.4 us (6%)
    all_to_all x1, waiting for transfers between devices, shards(): lax.all_to_all(stacked, 'patch', split_axis=1, concat_axis=2, tiled=True)  72.5 us
    dot_general x13, matrix products, attend_item(): jnp.dot(probs.astype(jnp.bfloat16), value_rows, preferred_element_type=jn...  45.4 us
    all_to_all x1, waiting for transfers between devices, shards(): lax.all_to_all(spatial_heads, 'patch', split_axis=1, concat_axis=0, tiled...  44 us
    reduce_sum x13, other arithmetic, attend_item(): total = jnp.sum(probs, axis=1, keepdims=True)  33.1 us
    dot_general x13, matrix products, attend_item(): jnp.einsum('qe,ke->qk', query, key_rows, preferred_element_type=jnp.float32)  29.1 us
    unnamed x15, local copies, waits for them, and re-layouts  19.3 us
    reshape x1, local copies, waits for them, and re-layouts, shards(): stacked = stacked.reshape(3, frames_dev * SH, cells_dev, HD)  14.7 us
    slice x8, local copies, waits for them, and re-layouts, attend_items(): return lax.map(single, (stacked[0], stacked[1], stacked[2], blocks))  10.8 us
  transfers between devices with their start and end apart: 4, of which 3 were waited for; matrix products, arithmetic and copies ran while one was open for 52% of the time, Pallas kernels for 0%

commit v1 on v0

v1 whole, which is shorter than its diff:
```python
import functools
import math

import jax
import jax.numpy as jnp
from jax import lax
from jax.experimental import pallas as pl
from jax.experimental.pallas import tpu as pltpu
from jax.sharding import PartitionSpec as P

HD = 128
SH = 28
TH = 12
GP = 32
BLOCK = 128
NF = 16
NP = 8
FD = 2
CELLS = 256
SEQ_S = NP * CELLS
SEQ_T = NF * FD * GP
NB_S = SEQ_S // BLOCK
NB_T = SEQ_T // BLOCK
ITEMS_S = FD * SH // NP
ITEMS_T = (CELLS // GP) * TH // NF
CHUNK = 2
CHUNKS = ITEMS_T // CHUNK
CW = CHUNK * HD
STAGES = ITEMS_S + CHUNKS
AHEAD = 3
TQ = 256
KC = 256
UNITS = 1.0 / math.sqrt(HD) * math.log2(math.e)
BIG = 1e30
MESH = pl.DeviceIdType.MESH


def attend(get_query, get_key, get_value, get_mask, put, first, length, scores_ref, value_ref):
    tiles = length // TQ
    halves = TQ // BLOCK
    for c in range(length // KC):
        value_ref[0:HD, c * KC : (c + 1) * KC] = get_value(c * KC, KC).T

    def step(d):
        tile = lax.rem(first + d, tiles)
        start = pl.multiple_of(tile * TQ, TQ)
        scaled = get_query(start, TQ).astype(jnp.float32) * UNITS
        high = scaled.astype(jnp.bfloat16)
        low = (scaled - high.astype(jnp.float32)).astype(jnp.bfloat16)
        query = jnp.concatenate([high, low], axis=1)

        def choose(j, rows, otherwise):
            parts = [
                jnp.where(
                    get_mask(tile * halves + i, j) > 0,
                    rows[:, i * BLOCK : (i + 1) * BLOCK],
                    otherwise,
                )
                for i in range(halves)
            ]
            return jnp.concatenate(parts, axis=1)

        top = jnp.full((8, TQ), -BIG, jnp.float32)
        for c in range(length // KC):
            key = get_key(c * KC, KC)
            scores = lax.dot_general(
                jnp.concatenate([key, key], axis=1),
                query,
                (((1,), (1,)), ((), ())),
                preferred_element_type=jnp.float32,
            )
            scores_ref[c * KC : (c + 1) * KC, :] = scores
            for b in range(KC // BLOCK):
                most = jnp.max(scores[b * BLOCK : (b + 1) * BLOCK].reshape(-1, 8, TQ), axis=0)
                top = jnp.maximum(top, choose(c * (KC // BLOCK) + b, most, -BIG))
        top = jnp.max(top, axis=0, keepdims=True)
        mixed = jnp.zeros((HD + 16, TQ), jnp.float32)
        for c in range(length // KC):
            parts = []
            for b in range(KC // BLOCK):
                j = c * (KC // BLOCK) + b
                shift = choose(j, top, BIG)
                parts.append(
                    jnp.exp2(scores_ref[j * BLOCK : (j + 1) * BLOCK, :] - shift).astype(jnp.bfloat16)
                )
            mixed = mixed + jnp.dot(
                value_ref[:, c * KC : (c + 1) * KC],
                jnp.concatenate(parts, axis=0),
                preferred_element_type=jnp.float32,
            )
        result = mixed[0:HD] * (1.0 / mixed[HD : HD + 1])
        put(tile, start, result.T.astype(jnp.bfloat16))

    pl.loop(0, tiles)(step)


def kernel(
    queries,
    keys,
    values,
    spatial_mask,
    temporal_mask,
    out,
    s_in,
    t_in,
    s_out,
    t_out,
    s_mask_in,
    t_mask_in,
    s_mask,
    t_mask,
    scores_ref,
    value_ref,
    mask_sem,
    in_recv,
    s_send,
    t_send,
    s_out_send,
    t_out_send,
    out_recv,
):
    me_f = lax.axis_index("frame")
    me_p = lax.axis_index("patch")
    tensors = (queries, keys, values)

    mask_copies = (
        pltpu.make_async_copy(
            spatial_mask.at[pl.ds(lax.rem(me_p, 4) * ITEMS_S, ITEMS_S)], s_mask_in, mask_sem.at[0]
        ),
        pltpu.make_async_copy(
            temporal_mask.at[pl.ds(lax.rem(me_f, 2) * ITEMS_T, ITEMS_T)], t_mask_in, mask_sem.at[1]
        ),
    )
    for copy in mask_copies:
        copy.start()

    barrier = pltpu.get_barrier_semaphore()

    @pl.loop(1, NP)
    def _(d):
        pl.semaphore_signal(
            barrier, inc=1, device_id=(me_f, lax.rem(me_p + d, NP)), device_id_type=MESH
        )

    @pl.loop(1, NF)
    def _(d):
        pl.semaphore_signal(
            barrier, inc=1, device_id=(lax.rem(me_f + d, NF), me_p), device_id_type=MESH
        )

    pl.semaphore_wait(barrier, NP + NF - 2)

    def spatial_place(rank, n):
        item = rank * ITEMS_S + n
        frame = item // SH
        return frame, pl.multiple_of((item - frame * SH) * HD, HD)

    def temporal_place(rank, c):
        group = rank // 2
        head = SH + (rank - group * 2) * ITEMS_T + c * CHUNK
        return pl.multiple_of(group * GP, GP), pl.multiple_of(head * HD, HD)

    def is_temporal(s):
        return lax.rem(s, 4) == 1

    def spatial_index(s):
        return s - (s + 2) // 4

    def start_spatial(s):
        n = spatial_index(s)

        def parts(rank):
            frame, column = spatial_place(rank, n)
            for i, tensor in enumerate(tensors):
                yield (
                    tensor.at[frame, :, pl.ds(column, HD)],
                    s_in.at[n, pl.ds(pl.multiple_of(i * SEQ_S + me_p * CELLS, CELLS), CELLS)],
                )

        @pl.loop(1, NP)
        def _(d):
            rank = lax.rem(me_p + d, NP)
            for source, target in parts(rank):
                pltpu.make_async_remote_copy(
                    src_ref=source,
                    dst_ref=target,
                    send_sem=s_send,
                    recv_sem=in_recv.at[s],
                    device_id=(me_f, rank),
                    device_id_type=MESH,
                ).start()

        for source, target in parts(me_p):
            pltpu.make_async_copy(source, target, in_recv.at[s]).start()

    def start_temporal(s):
        c = s // 4

        def parts(rank):
            row, column = temporal_place(rank, c)
            for i, tensor in enumerate(tensors):
                yield (
                    tensor.at[:, pl.ds(row, GP), pl.ds(column, CW)],
                    t_in.at[c, pl.ds(i * NF * FD + me_f * FD, FD)],
                )

        @pl.loop(1, NF)
        def _(d):
            rank = lax.rem(me_f + d, NF)
            for source, target in parts(rank):
                pltpu.make_async_remote_copy(
                    src_ref=source,
                    dst_ref=target,
                    send_sem=t_send,
                    recv_sem=in_recv.at[s],
                    device_id=(rank, me_p),
                    device_id_type=MESH,
                ).start()

        for source, target in parts(me_f):
            pltpu.make_async_copy(source, target, in_recv.at[s]).start()

    def start_stage(s):
        @pl.when(is_temporal(s))
        def _():
            start_temporal(s)

        @pl.when(jnp.logical_not(is_temporal(s)))
        def _():
            start_spatial(s)

    pl.loop(0, AHEAD)(start_stage)

    for copy in mask_copies:
        copy.wait()
    s_lane = me_f * FD + me_p // 4
    t_lane = me_p * (CELLS // GP) + me_f // 2

    def spread(rows, lane):
        lanes = lax.broadcasted_iota(jnp.int32, rows.shape, 2)
        chosen = jnp.sum(jnp.where(lanes == lane, rows.astype(jnp.float32), 0.0), axis=2, keepdims=True)
        return jnp.broadcast_to(chosen, rows.shape[:2] + (BLOCK,))

    @pl.loop(0, ITEMS_S)
    def _(n):
        s_mask[pl.ds(n * NB_S, NB_S)] = spread(s_mask_in[n], s_lane)

    @pl.loop(0, ITEMS_T)
    def _(n):
        t_mask[pl.ds(n * NB_T, NB_T)] = spread(t_mask_in[n], t_lane)

    value_ref[HD:, :] = jnp.ones((16, SEQ_S), jnp.bfloat16)

    def work_spatial(s):
        n = spatial_index(s)
        frame, column = spatial_place(me_p, n)
        pltpu.make_async_copy(s_in.at[n], s_in.at[n], in_recv.at[s]).wait()

        def put(tile, start, rows):
            s_out[n, pl.ds(start, TQ), :] = rows
            source = s_out.at[n, pl.ds(start, TQ)]
            target = out.at[frame, :, pl.ds(column, HD)]

            @pl.when(tile != me_p)
            def _():
                pltpu.make_async_remote_copy(
                    src_ref=source,
                    dst_ref=target,
                    send_sem=s_out_send,
                    recv_sem=out_recv,
                    device_id=(me_f, tile),
                    device_id_type=MESH,
                ).start()

            @pl.when(tile == me_p)
            def _():
                pltpu.make_async_copy(source, target, out_recv).start()

        attend(
            lambda a, l: s_in[n, pl.ds(a, l), :],
            lambda a, l: s_in[n, pl.ds(SEQ_S + a, l), :],
            lambda a, l: s_in[n, pl.ds(2 * SEQ_S + a, l), :],
            lambda i, j: s_mask[n * NB_S + i, j : j + 1, :],
            put,
            me_p + 1,
            SEQ_S,
            scores_ref,
            value_ref,
        )

    def work_temporal(s):
        c = s // 4
        pltpu.make_async_copy(t_in.at[c], t_in.at[c], in_recv.at[s]).wait()
        row, column = temporal_place(me_f, c)
        ranks = TQ // (FD * GP)

        @pl.loop(0, CHUNK)
        def _(h):
            lanes = pl.ds(pl.multiple_of(h * HD, HD), HD)

            def get(i):
                def rows(a, l):
                    if isinstance(a, int):
                        first = a // GP
                    else:
                        first = a // GP
                    return t_in[c, pl.ds(i * NF * FD + first, l // GP), :, lanes].reshape(l, HD)

                return rows

            def put(tile, start, rows):
                frame = tile * (TQ // GP)
                t_out[c, pl.ds(frame, TQ // GP), :, lanes] = rows.reshape(TQ // GP, GP, HD)
                target = out.at[
                    :, pl.ds(row, GP), pl.ds(pl.multiple_of(column + h * HD, HD), HD)
                ]

                for e in range(ranks):
                    rank = tile * ranks + e
                    source = t_out.at[c, pl.ds(rank * FD, FD), :, lanes]

                    @pl.when(rank != me_f)
                    def _():
                        pltpu.make_async_remote_copy(
                            src_ref=source,
                            dst_ref=target,
                            send_sem=t_out_send,
                            recv_sem=out_recv,
                            device_id=(rank, me_p),
                            device_id_type=MESH,
                        ).start()

                    @pl.when(rank == me_f)
                    def _():
                        pltpu.make_async_copy(source, target, out_recv).start()

            item = (c * CHUNK + h) * NB_T
            attend(
                get(0),
                get(1),
                get(2),
                lambda i, j: t_mask[item + i, j : j + 1, :],
                put,
                me_f // ranks + 1,
                SEQ_T,
                scores_ref,
                value_ref,
            )

    @pl.loop(0, STAGES)
    def _(s):
        @pl.when(s + AHEAD < STAGES)
        def _():
            start_stage(s + AHEAD)

        @pl.when(is_temporal(s))
        def _():
            work_temporal(s)

        @pl.when(jnp.logical_not(is_temporal(s)))
        def _():
            work_spatial(s)

    sent = (
        (s_in.at[:, pl.ds(0, 3 * (NP - 1) * CELLS)], s_send),
        (t_in.at[:, pl.ds(0, 3 * (NF - 1) * FD)], t_send),
        (s_out.at[:, pl.ds(0, (NP - 1) * CELLS)], s_out_send),
        (t_out.at[:, pl.ds(0, (NF - 1) * FD)], t_out_send),
        (out, out_recv),
    )
    for ref, sem in sent:
        pltpu.make_async_copy(ref, ref, sem).wait()


def shards(queries, keys, values, spatial_mask, temporal_mask):
    anywhere = pl.BlockSpec(memory_space=pl.ANY)
    dma = pltpu.SemaphoreType.DMA
    flops = 4 * HD * (ITEMS_S * SEQ_S**2 + ITEMS_T * SEQ_T**2)
    return pl.pallas_call(
        kernel,
        out_shape=jax.ShapeDtypeStruct(queries.shape, queries.dtype),
        in_specs=[anywhere] * 5,
        out_specs=anywhere,
        scratch_shapes=[
            pltpu.VMEM((ITEMS_S, 3 * SEQ_S, HD), jnp.bfloat16),
            pltpu.VMEM((CHUNKS, 3 * NF * FD, GP, CW), jnp.bfloat16),
            pltpu.VMEM((ITEMS_S, SEQ_S, HD), jnp.bfloat16),
            pltpu.VMEM((CHUNKS, NF * FD, GP, CW), jnp.bfloat16),
            pltpu.VMEM((ITEMS_S, NB_S, NB_S, 32), jnp.int32),
            pltpu.VMEM((ITEMS_T, NB_T, NB_T, 64), jnp.int32),
            pltpu.VMEM((ITEMS_S * NB_S, NB_S, BLOCK), jnp.float32),
            pltpu.VMEM((ITEMS_T * NB_T, NB_T, BLOCK), jnp.float32),
            pltpu.VMEM((SEQ_S, TQ), jnp.float32),
            pltpu.VMEM((HD + 16, SEQ_S), jnp.bfloat16),
            dma((2,)),
            dma((STAGES,)),
            dma,
            dma,
            dma,
            dma,
            dma,
        ],
        compiler_params=pltpu.CompilerParams(
            collective_id=0, has_side_effects=True, vmem_limit_bytes=60 * 2**20
        ),
        cost_estimate=pl.CostEstimate(
            flops=flops, bytes_accessed=4 * queries.size * 2, transcendentals=flops // (4 * HD)
        ),
    )(
        queries,
        keys,
        values,
        spatial_mask.transpose(1, 2, 3, 0),
        temporal_mask.transpose(1, 2, 3, 0),
    )


def solution(mesh):
    in_specs = (
        P("frame", "patch", None),
        P("frame", "patch", None),
        P("frame", "patch", None),
        P(),
        P(),
    )
    out_specs = P("frame", "patch", None)
    return jax.shard_map(shards, mesh=mesh, in_specs=in_specs, out_specs=out_specs, check_vma=False)
```

time: 409 us -> 244 us (0.60)
  Pallas kernels: 0 us -> 237 us
  local copies, waits for them, and re-layouts: 134 us -> 5.18 us
  waiting for transfers between devices: 120 us -> 0 us
  matrix products: 74.5 us -> 0 us
  other arithmetic: 52.1 us -> 0 us
  starting transfers between devices: 24.4 us -> 0 us
    pallas_call x0 -> x1, Pallas kernels: none -> 237 us  [shards(): pl.pallas_call(kernel, out_shape=jax.ShapeDtypeStruct(queries.shape, quer...]
    all_to_all x4 -> x0, waiting for transfers between devices: 120 us -> none  [the longest x1 72.5 us: shards(): lax.all_to_all(stacked, 'patch', split_axis=1, concat_axis=2, tiled=True)]
    dot_general x26 -> x0, matrix products: 74.5 us -> none  [the longest x13 45.4 us: attend_item(): jnp.dot(probs.astype(jnp.bfloat16), value_rows, preferred_element_type=jn...]
    reduce_sum x13 -> x0, other arithmetic: 33.1 us -> none  [attend_item(): total = jnp.sum(probs, axis=1, keepdims=True)]
    slice x14 -> x0, local copies, waits for them, and re-layouts: 29.4 us -> none  [the longest x8 10.8 us: attend_items(): return lax.map(single, (stacked[0], stacked[1], stacked[2], blocks))]
    reshape x12 -> x0, local copies, waits for them, and re-layouts: 27.6 us -> none  [the longest x1 14.7 us: shards(): stacked = stacked.reshape(3, frames_dev * SH, cells_dev, HD)]
    all_to_all x4 -> x0, starting transfers between devices: 24.4 us -> none  [the longest x1 8.58 us: shards(): lax.all_to_all(packed, 'frame', split_axis=1, concat_axis=2, tiled=True)]
    all_to_all x4 -> x0, local copies, waits for them, and re-layouts: 15.1 us -> none  [the longest x1 6.22 us: shards(): lax.all_to_all(stacked, 'patch', split_axis=1, concat_axis=2, tiled=True)]
  transfers between devices with their start and end apart: 4 -> 0, of which waited for: 3 -> 0; matrix products, arithmetic and copies ran while one was open for 52% -> 0% of each run, Pallas kernels for 0% -> 0%
where the time goes in v1:
time: 244 us; the launch traced here: 242 us
  Pallas kernels  237 us (97%)
  local copies, waits for them, and re-layouts  5.18 us (2%)
    pallas_call x1, Pallas kernels, shards(): pl.pallas_call(kernel, out_shape=jax.ShapeDtypeStruct(queries.shape, quer...  237 us
    unnamed x1, local copies, waits for them, and re-layouts  5.18 us

profile of v1, /device:TPU:1, one launch (start us, length us, event | category | flops | bytes accessed | tf_op | source)
XLA Modules:
  0.0 242.5 jit_solution(18216379477103774381)
XLA Ops:
  0.0 237.3 %shard_map.55 = bf16[2,256,5120]{2,1,0:T(8,128)(2,1)} custom-call(bf16[2,256,5120]{2,1,0:T(8,128)(2,1)} %queries.1, bf16[2,256,5120]{2,1,0:T(8,128)(2,1)} %keys.1, bf16[2,256,5120]{2,1,0:T(8,128)(2,1)} %values.1, s32[28,16,16,32]{3,2,1,0:T(8,128)} %bitcast.2, s32[12,8,8,64]{3,2,1,0:T(8,128)} %bitcast.3), custom_call_target="tpu_custom_call" | custom-call | flops 18253611008 | bytes 20971520 | tf_op jit(solution)/shard_map/pallas_call | solution.py:379
  237.3 5.2 %copy.7 = bf16[2,256,5120]{2,1,0:T(8,128)(2,1)} copy(bf16[2,256,5120]{2,1,0:T(8,128)(2,1)} %shard_map.55) | data formatting | bytes 10485760

commit v2 on v1

--- a/solution.py
+++ b/solution.py
@@ -27,7 +27,7 @@
 CHUNKS = ITEMS_T // CHUNK
 CW = CHUNK * HD
 STAGES = ITEMS_S + CHUNKS
-AHEAD = 3
+AHEAD = 5
 TQ = 256
 KC = 256
 UNITS = 1.0 / math.sqrt(HD) * math.log2(math.e)
@@ -374,12 +374,13 @@
 
 def shards(queries, keys, values, spatial_mask, temporal_mask):
     anywhere = pl.BlockSpec(memory_space=pl.ANY)
+    held = pl.BlockSpec(memory_space=pltpu.HBM)
     dma = pltpu.SemaphoreType.DMA
     flops = 4 * HD * (ITEMS_S * SEQ_S**2 + ITEMS_T * SEQ_T**2)
     return pl.pallas_call(
         kernel,
-        out_shape=jax.ShapeDtypeStruct(queries.shape, queries.dtype),
-        in_specs=[anywhere] * 5,
+        out_shape=pltpu.VMEM(queries.shape, queries.dtype),
+        in_specs=[held] * 5,
         out_specs=anywhere,
         scratch_shapes=[
             pltpu.VMEM((ITEMS_S, 3 * SEQ_S, HD), jnp.bfloat16),
@@ -401,7 +402,7 @@
             dma,
         ],
         compiler_params=pltpu.CompilerParams(
-            collective_id=0, has_side_effects=True, vmem_limit_bytes=60 * 2**20
+            collective_id=0, has_side_effects=True, vmem_limit_bytes=50 * 2**20
         ),
         cost_estimate=pl.CostEstimate(
             flops=flops, bytes_accessed=4 * queries.size * 2, transcendentals=flops // (4 * HD)

time: 244 us -> 240 us (0.984)
  local copies, waits for them, and re-layouts: 5.18 us -> 2.36 us
    unnamed x1, local copies, waits for them, and re-layouts: 5.18 us -> 2.36 us
where the time goes in v2:
time: 240 us; the launch traced here: 239 us
  Pallas kernels  237 us (99%)
    pallas_call x1, Pallas kernels, shards(): pl.pallas_call(kernel, out_shape=pltpu.VMEM(queries.shape, queries.dtype)...  237 us

profile of v2, /device:TPU:1, one launch (start us, length us, event | category | flops | bytes accessed | tf_op | source)
XLA Modules:
  0.0 239.3 jit_solution(1370782008219324000)
XLA Ops:
  0.0 236.9 %shard_map.55 = bf16[2,256,5120]{2,1,0:T(8,128)(2,1)S(1)} custom-call(bf16[2,256,5120]{2,1,0:T(8,128)(2,1)} %queries.1, bf16[2,256,5120]{2,1,0:T(8,128)(2,1)} %keys.1, bf16[2,256,5120]{2,1,0:T(8,128)(2,1)} %values.1, s32[28,16,16,32]{3,2,1,0:T(8,128)} %bitcast.2, s32[12,8,8,64]{3,2,1,0:T(8,128)} %bitcast.3), custom_call_target="tpu_custom_call" | custom-call | flops 18253611008 | bytes 20971520 | tf_op jit(solution)/shard_map/pallas_call | solution.py:380
  236.9 2.4 copy.7

commit v3 on v2

--- a/solution.py
+++ b/solution.py
@@ -27,6 +27,7 @@
 CHUNKS = ITEMS_T // CHUNK
 CW = CHUNK * HD
 STAGES = ITEMS_S + CHUNKS
+HOLD = 4
 AHEAD = 5
 TQ = 256
 KC = 256
@@ -251,29 +252,41 @@
 
     value_ref[HD:, :] = jnp.ones((16, SEQ_S), jnp.bfloat16)
 
+    beside = me_p + 1 - 2 * lax.rem(me_p, 2)
+
+    def spatial_rows(n, rank):
+        frame, column = spatial_place(me_p, n)
+        return (
+            s_out.at[n, pl.ds(pl.multiple_of(rank * CELLS, CELLS), CELLS)],
+            out.at[frame, :, pl.ds(column, HD)],
+        )
+
+    def give_spatial(n, rank):
+        source, target = spatial_rows(n, rank)
+        pltpu.make_async_remote_copy(
+            src_ref=source,
+            dst_ref=target,
+            send_sem=s_out_send,
+            recv_sem=out_recv,
+            device_id=(me_f, rank),
+            device_id_type=MESH,
+        ).start()
+
     def work_spatial(s):
         n = spatial_index(s)
-        frame, column = spatial_place(me_p, n)
         pltpu.make_async_copy(s_in.at[n], s_in.at[n], in_recv.at[s]).wait()
 
         def put(tile, start, rows):
             s_out[n, pl.ds(start, TQ), :] = rows
-            source = s_out.at[n, pl.ds(start, TQ)]
-            target = out.at[frame, :, pl.ds(column, HD)]
-
-            @pl.when(tile != me_p)
+            held = (tile == beside) & (n >= ITEMS_S - HOLD)
+
+            @pl.when((tile != me_p) & jnp.logical_not(held))
             def _():
-                pltpu.make_async_remote_copy(
-                    src_ref=source,
-                    dst_ref=target,
-                    send_sem=s_out_send,
-                    recv_sem=out_recv,
-                    device_id=(me_f, tile),
-                    device_id_type=MESH,
-                ).start()
+                give_spatial(n, tile)
 
             @pl.when(tile == me_p)
             def _():
+                source, target = spatial_rows(n, tile)
                 pltpu.make_async_copy(source, target, out_recv).start()
 
         attend(
@@ -300,11 +313,7 @@
 
             def get(i):
                 def rows(a, l):
-                    if isinstance(a, int):
-                        first = a // GP
-                    else:
-                        first = a // GP
-                    return t_in[c, pl.ds(i * NF * FD + first, l // GP), :, lanes].reshape(l, HD)
+                    return t_in[c, pl.ds(i * NF * FD + a // GP, l // GP), :, lanes].reshape(l, HD)
 
                 return rows
 
@@ -360,6 +369,10 @@
         @pl.when(jnp.logical_not(is_temporal(s)))
         def _():
             work_spatial(s)
+
+    @pl.loop(ITEMS_S - HOLD, ITEMS_S)
+    def _(n):
+        give_spatial(n, beside)
 
     sent = (
         (s_in.at[:, pl.ds(0, 3 * (NP - 1) * CELLS)], s_send),

time: 240 us -> 239 us (level)
  no operation moved by 1% of the time
where the time goes in v3:
time: 239 us
  Pallas kernels  236 us (99%)
    pallas_call x1, Pallas kernels, shards(): pl.pallas_call(kernel, out_shape=pltpu.VMEM(queries.shape, queries.dtype)...  236 us

profile of v3, /device:TPU:1, one launch (start us, length us, event | category | flops | bytes accessed | tf_op | source)
XLA Modules:
  0.0 238.8 jit_solution(1031629758235512087)
XLA Ops:
  0.0 236.4 %shard_map.55 = bf16[2,256,5120]{2,1,0:T(8,128)(2,1)S(1)} custom-call(bf16[2,256,5120]{2,1,0:T(8,128)(2,1)} %queries.1, bf16[2,256,5120]{2,1,0:T(8,128)(2,1)} %keys.1, bf16[2,256,5120]{2,1,0:T(8,128)(2,1)} %values.1, s32[28,16,16,32]{3,2,1,0:T(8,128)} %bitcast.2, s32[12,8,8,64]{3,2,1,0:T(8,128)} %bitcast.3), custom_call_target="tpu_custom_call" | custom-call | flops 18253611008 | bytes 20971520 | tf_op jit(solution)/shard_map/pallas_call | solution.py:393
  236.4 2.4 copy.7

commit v4 on v3

--- a/solution.py
+++ b/solution.py
@@ -27,7 +27,7 @@
 CHUNKS = ITEMS_T // CHUNK
 CW = CHUNK * HD
 STAGES = ITEMS_S + CHUNKS
-HOLD = 4
+HOLD = 7
 AHEAD = 5
 TQ = 256
 KC = 256
@@ -36,14 +36,14 @@
 MESH = pl.DeviceIdType.MESH
 
 
-def attend(get_query, get_key, get_value, get_mask, put, first, length, scores_ref, value_ref):
+def attend(get_query, get_key, get_value, get_mask, put, first, order, length, scores_ref, value_ref):
     tiles = length // TQ
     halves = TQ // BLOCK
     for c in range(length // KC):
         value_ref[0:HD, c * KC : (c + 1) * KC] = get_value(c * KC, KC).T
 
     def step(d):
-        tile = lax.rem(first + d, tiles)
+        tile = lax.rem(first + order(d), tiles)
         start = pl.multiple_of(tile * TQ, TQ)
         scaled = get_query(start, TQ).astype(jnp.float32) * UNITS
         high = scaled.astype(jnp.bfloat16)
@@ -296,6 +296,7 @@
             lambda i, j: s_mask[n * NB_S + i, j : j + 1, :],
             put,
             me_p + 1,
+            lambda d: d,
             SEQ_S,
             scores_ref,
             value_ref,
@@ -351,6 +352,7 @@
                 lambda i, j: t_mask[item + i, j : j + 1, :],
                 put,
                 me_f // ranks + 1,
+                lambda d: jnp.where(d < 2, 1 - d, d),
                 SEQ_T,
                 scores_ref,
                 value_ref,

time: 239 us -> 239 us (level)
  no operation moved by 1% of the time
where the time goes in v4:
time: 239 us
  Pallas kernels  236 us (99%)
    pallas_call x1, Pallas kernels, shards(): pl.pallas_call(kernel, out_shape=pltpu.VMEM(queries.shape, queries.dtype)...  236 us

profile of v4, /device:TPU:1, one launch (start us, length us, event | category | flops | bytes accessed | tf_op | source)
XLA Modules:
  0.0 238.7 jit_solution(602470524887672539)
XLA Ops:
  0.0 236.3 %shard_map.55 = bf16[2,256,5120]{2,1,0:T(8,128)(2,1)S(1)} custom-call(bf16[2,256,5120]{2,1,0:T(8,128)(2,1)} %queries.1, bf16[2,256,5120]{2,1,0:T(8,128)(2,1)} %keys.1, bf16[2,256,5120]{2,1,0:T(8,128)(2,1)} %values.1, s32[28,16,16,32]{3,2,1,0:T(8,128)} %bitcast.2, s32[12,8,8,64]{3,2,1,0:T(8,128)} %bitcast.3), custom_call_target="tpu_custom_call" | custom-call | flops 18253611008 | bytes 20971520 | tf_op jit(solution)/shard_map/pallas_call | solution.py:395
  236.3 2.4 copy.7

commit v5 on v3

--- a/solution.py
+++ b/solution.py
@@ -124,6 +124,21 @@
     me_p = lax.axis_index("patch")
     tensors = (queries, keys, values)
 
+    barrier = pltpu.get_barrier_semaphore()
+
+    @pl.loop(0, NF - 1)
+    def _(k):
+        d = jnp.where(k < NF // 2, k + NF // 2, k + 1 - NF // 2)
+        pl.semaphore_signal(
+            barrier, inc=1, device_id=(lax.rem(me_f + d, NF), me_p), device_id_type=MESH
+        )
+
+    @pl.loop(1, NP)
+    def _(d):
+        pl.semaphore_signal(
+            barrier, inc=1, device_id=(me_f, lax.rem(me_p + d, NP)), device_id_type=MESH
+        )
+
     mask_copies = (
         pltpu.make_async_copy(
             spatial_mask.at[pl.ds(lax.rem(me_p, 4) * ITEMS_S, ITEMS_S)], s_mask_in, mask_sem.at[0]
@@ -134,20 +149,6 @@
     )
     for copy in mask_copies:
         copy.start()
-
-    barrier = pltpu.get_barrier_semaphore()
-
-    @pl.loop(1, NP)
-    def _(d):
-        pl.semaphore_signal(
-            barrier, inc=1, device_id=(me_f, lax.rem(me_p + d, NP)), device_id_type=MESH
-        )
-
-    @pl.loop(1, NF)
-    def _(d):
-        pl.semaphore_signal(
-            barrier, inc=1, device_id=(lax.rem(me_f + d, NF), me_p), device_id_type=MESH
-        )
 
     pl.semaphore_wait(barrier, NP + NF - 2)
 

time: 239 us -> 239 us (level)
  no operation moved by 1% of the time
where the time goes in v5:
time: 239 us
  Pallas kernels  237 us (99%)
    pallas_call x1, Pallas kernels, shards(): pl.pallas_call(kernel, out_shape=pltpu.VMEM(queries.shape, queries.dtype)...  237 us

profile of v5, /device:TPU:1, one launch (start us, length us, event | category | flops | bytes accessed | tf_op | source)
XLA Modules:
  0.0 239.0 jit_solution(5841246782883624448)
XLA Ops:
  0.0 236.6 %shard_map.55 = bf16[2,256,5120]{2,1,0:T(8,128)(2,1)S(1)} custom-call(bf16[2,256,5120]{2,1,0:T(8,128)(2,1)} %queries.1, bf16[2,256,5120]{2,1,0:T(8,128)(2,1)} %keys.1, bf16[2,256,5120]{2,1,0:T(8,128)(2,1)} %values.1, s32[28,16,16,32]{3,2,1,0:T(8,128)} %bitcast.2, s32[12,8,8,64]{3,2,1,0:T(8,128)} %bitcast.3), custom_call_target="tpu_custom_call" | custom-call | flops 18253611008 | bytes 20971520 | tf_op jit(solution)/shard_map/pallas_call | solution.py:394
  236.6 2.4 copy.7
